TPU v7x, 32 devices: a whole 2x2x4 slice. The times are simulated.
32 devices in a mesh: ctx: 4 (over z), head: 8 (over y, x, core).
Axes of the slice: x: 2, y: 2, z: 4, core: 2. Of those that a mesh axis runs over, the one named last changes fastest.
Arguments:
- queries: bfloat16 [8192, 4096], P(('ctx', 'head')), may hold values from -8 to 8
- keys: bfloat16 [8192, 2048], P(('ctx', 'head')), may hold values from -8 to 8
- values: bfloat16 [8192, 2048], P(('ctx', 'head')), may hold values from -18 to 18
- grad_out: bfloat16 [8192, 4096], P(('ctx', 'head')), may hold values from -18 to 18
Outputs:
- attended: bfloat16 [8192, 4096], P(('ctx', 'head'))
- grad_queries: bfloat16 [8192, 4096], P(('ctx', 'head'))
- grad_keys: bfloat16 [8192, 2048], P(('ctx', 'head'))
- grad_values: bfloat16 [8192, 2048], P(('ctx', 'head'))
All inputs are finite; a program needn't handle non-finite values.
Results may differ from a plain program's by a relative error of at most 0.02.
Values may be sent and summed in bfloat16 or wider, within the bound.
A program may use at most 256 MiB of HBM per device.

v0:
```python
import jax
import jax.numpy as jnp
from jax import lax
from jax.sharding import PartitionSpec as P

HD = 128
QH = 32
KVH = 16
WIN = 1024
QPRE = 168
BLK = 256


def shifted(block, axis, distance):
    devices = range(lax.axis_size(axis))
    route = [(i - distance, i) for i in devices if i - distance in devices]
    return lax.ppermute(block, axis, route)


def place_blocks(stacked, reach):
    block_total = stacked.shape[0]
    shared_heads = stacked.shape[1]
    block_rows = stacked.shape[3]
    head_width = stacked.shape[4]
    total = None
    for offset in range(reach + 1):
        piece = stacked[:, :, offset]
        padded = jnp.pad(piece, ((offset, reach - offset), (0, 0), (0, 0), (0, 0)))
        total = padded if total is None else total + padded
    total = jnp.transpose(total, (0, 2, 1, 3))
    return total.reshape((block_total + reach) * block_rows, shared_heads, head_width)


def attend(queries, keys_ext, values_ext, grads, first_query):
    query_count = queries.shape[0]
    query_heads = queries.shape[1]
    shared_heads = keys_ext.shape[1]
    head_width = queries.shape[2]
    group_size = query_heads // shared_heads
    block_rows = min(BLK, query_count)
    reach = WIN // block_rows
    key_span = WIN + block_rows
    block_total = query_count // block_rows
    scale = QPRE ** (-0.5)
    query_major = jnp.transpose(
        queries.reshape(query_count, shared_heads, group_size, head_width), (1, 2, 0, 3)
    )
    grad_major = jnp.transpose(
        grads.reshape(query_count, shared_heads, group_size, head_width), (1, 2, 0, 3)
    )
    key_major = jnp.transpose(keys_ext, (1, 0, 2))
    value_major = jnp.transpose(values_ext, (1, 0, 2))

    def block_step(carry, block):
        first_row = block * block_rows
        query_stack = lax.dynamic_slice_in_dim(query_major, first_row, block_rows, 2)
        grad_stack = lax.dynamic_slice_in_dim(grad_major, first_row, block_rows, 2)
        key_stack = lax.dynamic_slice_in_dim(key_major, first_row, key_span, 1)
        value_stack = lax.dynamic_slice_in_dim(value_major, first_row, key_span, 1)
        query_pos = first_query + first_row + jnp.arange(block_rows, dtype=jnp.int32)
        key_pos = first_query - WIN + first_row + jnp.arange(key_span, dtype=jnp.int32)
        distance = query_pos[:, None] - key_pos[None, :]
        allowed = (distance >= 0) & (distance < WIN) & (key_pos[None, :] >= 0)
        scores = (
            jnp.einsum("sgqd,skd->sgqk", query_stack, key_stack, preferred_element_type=jnp.float32)
            * scale
        )
        scores = jnp.where(allowed[None, None], scores, -jnp.inf)
        largest = jnp.max(scores, axis=-1, keepdims=True)
        unnormed = jnp.exp(scores - largest)
        probs = unnormed / jnp.sum(unnormed, axis=-1, keepdims=True)
        probs_low = probs.astype(jnp.bfloat16)
        output_stack = jnp.einsum(
            "sgqk,skd->sgqd", probs_low, value_stack, preferred_element_type=jnp.float32
        ).astype(jnp.bfloat16)
        grad_probs = jnp.einsum(
            "sgqd,skd->sgqk", grad_stack, value_stack, preferred_element_type=jnp.float32
        )
        inner = jnp.sum(
            grad_stack.astype(jnp.float32) * output_stack.astype(jnp.float32),
            axis=-1,
            keepdims=True,
        )
        grad_scores = (probs * (grad_probs - inner) * scale).astype(jnp.bfloat16)
        grad_query = jnp.einsum(
            "sgqk,skd->sgqd", grad_scores, key_stack, preferred_element_type=jnp.float32
        ).astype(jnp.bfloat16)
        grad_key = jnp.einsum(
            "sgqk,sgqd->skd", grad_scores, query_stack, preferred_element_type=jnp.float32
        )
        grad_value = jnp.einsum(
            "sgqk,sgqd->skd", probs_low, grad_stack, preferred_element_type=jnp.float32
        )
        return (carry, (output_stack, grad_query, grad_key, grad_value))

    unused, (outputs, grad_queries, key_terms, value_terms) = lax.scan(
        block_step, None, jnp.arange(block_total, dtype=jnp.int32)
    )
    attended = jnp.transpose(outputs, (0, 3, 1, 2, 4)).reshape(query_count, query_heads, head_width)
    grad_queries = jnp.transpose(grad_queries, (0, 3, 1, 2, 4)).reshape(
        query_count, query_heads, head_width
    )
    key_terms = key_terms.reshape(block_total, shared_heads, reach + 1, block_rows, head_width)
    value_terms = value_terms.reshape(block_total, shared_heads, reach + 1, block_rows, head_width)
    key_total = place_blocks(key_terms, reach)
    value_total = place_blocks(value_terms, reach)
    return (attended, grad_queries, key_total, value_total)


def body(queries, keys, values, grad_out):
    token_count = queries.shape[0]
    query_rows = queries.reshape(token_count, QH, HD)
    key_rows = keys.reshape(token_count, KVH, HD)
    value_rows = values.reshape(token_count, KVH, HD)
    grad_rows = grad_out.reshape(token_count, QH, HD)
    group_queries, group_keys, group_values, group_grads = (
        lax.all_to_all(query_rows, "head", split_axis=1, concat_axis=0, tiled=True),
        lax.all_to_all(key_rows, "head", split_axis=1, concat_axis=0, tiled=True),
        lax.all_to_all(value_rows, "head", split_axis=1, concat_axis=0, tiled=True),
        lax.all_to_all(grad_rows, "head", split_axis=1, concat_axis=0, tiled=True),
    )
    group_rows = group_queries.shape[0]
    first_query = lax.axis_index("ctx") * group_rows
    key_tail, value_tail = shifted(
        (group_keys[group_rows - WIN :], group_values[group_rows - WIN :]), "ctx", 1
    )
    keys_ext = jnp.concatenate([key_tail, group_keys], axis=0)
    values_ext = jnp.concatenate([value_tail, group_values], axis=0)
    attended_group, grad_query_group, key_total, value_total = attend(
        group_queries, keys_ext, values_ext, group_grads, first_query
    )
    key_back, value_back = (
        shifted(key_total[:WIN].astype(jnp.bfloat16), "ctx", -1).astype(jnp.float32),
        shifted(value_total[:WIN].astype(jnp.bfloat16), "ctx", -1).astype(jnp.float32),
    )
    key_grad = jnp.concatenate(
        [key_total[WIN:group_rows], key_total[group_rows:] + key_back], axis=0
    ).astype(jnp.bfloat16)
    value_grad = jnp.concatenate(
        [value_total[WIN:group_rows], value_total[group_rows:] + value_back], axis=0
    ).astype(jnp.bfloat16)
    attended, grad_queries, key_out, value_out = (
        lax.all_to_all(attended_group, "head", split_axis=0, concat_axis=1, tiled=True),
        lax.all_to_all(grad_query_group, "head", split_axis=0, concat_axis=1, tiled=True),
        lax.all_to_all(key_grad, "head", split_axis=0, concat_axis=1, tiled=True),
        lax.all_to_all(value_grad, "head", split_axis=0, concat_axis=1, tiled=True),
    )
    return (
        attended.reshape(token_count, QH * HD),
        grad_queries.reshape(token_count, QH * HD),
        key_out.reshape(token_count, KVH * HD),
        value_out.reshape(token_count, KVH * HD),
    )


def solution(mesh):
    placed = (
        P(("ctx", "head"), None),
        P(("ctx", "head"), None),
        P(("ctx", "head"), None),
        P(("ctx", "head"), None),
    )
    return jax.shard_map(
        body,
        mesh=mesh,
        in_specs=placed,
        out_specs=(
            P(("ctx", "head"), None),
            P(("ctx", "head"), None),
            P(("ctx", "head"), None),
            P(("ctx", "head"), None),
        ),
        check_vma=False,
    )
```

profile of v0, /device:TPU:7, one launch (start us, length us, event | category | flops | bytes accessed | tf_op | source)
XLA Modules:
  0.0 467.4 jit_solution(16434716455477512644)
XLA Ops:
  8.8 11.4 %all-to-all-done.1 = bf16[256,16,128]{0,2,1:T(8,128)(2,1)S(1)} async-done(((bf16[256,16,128]{0,2,1:T(8,128)(2,1)}), bf16[256,16,128]{0,2,1:T(8,128)(2,1)S(1)}, u32[]{:S(2)}, u32[]{:S(2)}) %all-to-all-start.1) | async-done | bytes 1048608 | tf_op jit(solution)/shard_map/all_to_all | solution.py:118
  20.2 6.2 %all-to-all-start.2 = ((bf16[256,16,128]{0,2,1:T(8,128)(2,1)}), bf16[256,16,128]{0,2,1:T(8,128)(2,1)S(1)}, u32[]{:S(2)}, u32[]{:S(2)}) async-start(bf16[256,16,128]{0,2,1:T(8,128)(2,1)} %bitcast.29), calls=%async_computation.2 | async-start | bytes 2097152 | tf_op jit(solution)/shard_map/all_to_all | solution.py:119
  30.5 8.6 %all-to-all-done.2 = bf16[256,16,128]{0,2,1:T(8,128)(2,1)S(1)} async-done(((bf16[256,16,128]{0,2,1:T(8,128)(2,1)}), bf16[256,16,128]{0,2,1:T(8,128)(2,1)S(1)}, u32[]{:S(2)}, u32[]{:S(2)}) %all-to-all-start.2) | async-done | bytes 1048608 | tf_op jit(solution)/shard_map/all_to_all | solution.py:119
  39.1 7.0 %all-to-all-start = ((bf16[256,32,128]{0,2,1:T(8,128)(2,1)}), bf16[256,32,128]{0,2,1:T(8,128)(2,1)}, u32[]{:S(2)}, u32[]{:S(2)}) async-start(bf16[256,32,128]{0,2,1:T(8,128)(2,1)} %bitcast.201), calls=%async_computation | async-start | bytes 4194304 | tf_op jit(solution)/shard_map/all_to_all | solution.py:117
  50.1 20.0 %all-to-all-done = bf16[256,32,128]{0,2,1:T(8,128)(2,1)} async-done(((bf16[256,32,128]{0,2,1:T(8,128)(2,1)}), bf16[256,32,128]{0,2,1:T(8,128)(2,1)}, u32[]{:S(2)}, u32[]{:S(2)}) %all-to-all-start) | async-done | bytes 2097184 | tf_op jit(solution)/shard_map/all_to_all | solution.py:117
  70.1 7.0 %all-to-all-start.3 = ((bf16[256,32,128]{0,2,1:T(8,128)(2,1)}), bf16[256,32,128]{0,2,1:T(8,128)(2,1)}, u32[]{:S(2)}, u32[]{:S(2)}) async-start(bf16[256,32,128]{0,2,1:T(8,128)(2,1)} %bitcast.200), calls=%async_computation.3 | async-start | bytes 4194304 | tf_op jit(solution)/shard_map/all_to_all | solution.py:120
  94.6 9.8 %collective-permute-done.1 = bf16[1024,2,128]{2,0,1:T(8,128)(2,1)} collective-permute-done((bf16[1024,2,128]{2,0,1:T(8,128)(2,1)}, bf16[1024,2,128]{2,0,1:T(8,128)(2,1)}, u32[]{:S(2)}, u32[]{:S(2)}) %collective-permute-start.1) | collective-permute-done | bytes 524320 | tf_op jit(solution)/shard_map/ppermute | solution.py:17
  114.5 205.1 %while.18 = (s32[]{:T(128)}, bf16[8,2,2,256,128]{4,3,0,2,1:T(8,128)(2,1)}, bf16[8,2,2,256,128]{4,3,0,2,1:T(8,128)(2,1)}, f32[8,2,1280,128]{3,2,1,0:T(8,128)}, f3...) while((s32[]{:T(128)}, ...), condition=%wide.region_4.5_spmd, body=%wide.region_0.4_spmd.sunk | while | flops 2030113024 | bytes 91655112 | solution.py:96
  117.4 5.1 %exponential_reduce_fusion.2 = (f32[2,2,256]{2,1,0:T(2,128)S(1)}, f32[2,2,256,1280]{3,2,1,0:T(8,128)}) fusion(pred[256,1280]{1,0:T(8,128)(4,1)S(1)} %fusion.80, bf16[2,3072,128]{2,1,0:T(8,128)(2,1)S(1)} %get-tuple-element.369, s32[]{:T(128)S(6)} %select_n.30, bf16[2,2,2048,128]{3,2,1,0:T(8,128)(2,1)} %get-tuple-element.368, s32[]{:T(128)S(6)} %select_n.29), kind=kOutput, calls=%fused_computation.5.clone.1 | convolution fusion | flops 340788480 | bytes 6492168 | tf_op jit(solution)/shard_map/while/body/eval_jaxpr/sub | solution.py:70
  143.0 5.1 %exponential_reduce_fusion.2 = (f32[2,2,256]{2,1,0:T(2,128)S(1)}, f32[2,2,256,1280]{3,2,1,0:T(8,128)}) fusion(pred[256,1280]{1,0:T(8,128)(4,1)S(1)} %fusion.80, bf16[2,3072,128]{2,1,0:T(8,128)(2,1)S(1)} %get-tuple-element.369, s32[]{:T(128)S(6)} %select_n.30, bf16[2,2,2048,128]{3,2,1,0:T(8,128)(2,1)} %get-tuple-element.368, s32[]{:T(128)S(6)} %select_n.29), kind=kOutput, calls=%fused_computation.5.clone.1 | convolution fusion | flops 340788480 | bytes 6492168 | tf_op jit(solution)/shard_map/while/body/eval_jaxpr/sub | solution.py:70
  168.6 5.1 %exponential_reduce_fusion.2 = (f32[2,2,256]{2,1,0:T(2,128)S(1)}, f32[2,2,256,1280]{3,2,1,0:T(8,128)}) fusion(pred[256,1280]{1,0:T(8,128)(4,1)S(1)} %fusion.80, bf16[2,3072,128]{2,1,0:T(8,128)(2,1)S(1)} %get-tuple-element.369, s32[]{:T(128)S(6)} %select_n.30, bf16[2,2,2048,128]{3,2,1,0:T(8,128)(2,1)} %get-tuple-element.368, s32[]{:T(128)S(6)} %select_n.29), kind=kOutput, calls=%fused_computation.5.clone.1 | convolution fusion | flops 340788480 | bytes 6492168 | tf_op jit(solution)/shard_map/while/body/eval_jaxpr/sub | solution.py:70
  194.2 5.1 %exponential_reduce_fusion.2 = (f32[2,2,256]{2,1,0:T(2,128)S(1)}, f32[2,2,256,1280]{3,2,1,0:T(8,128)}) fusion(pred[256,1280]{1,0:T(8,128)(4,1)S(1)} %fusion.80, bf16[2,3072,128]{2,1,0:T(8,128)(2,1)S(1)} %get-tuple-element.369, s32[]{:T(128)S(6)} %select_n.30, bf16[2,2,2048,128]{3,2,1,0:T(8,128)(2,1)} %get-tuple-element.368, s32[]{:T(128)S(6)} %select_n.29), kind=kOutput, calls=%fused_computation.5.clone.1 | convolution fusion | flops 340788480 | bytes 6492168 | tf_op jit(solution)/shard_map/while/body/eval_jaxpr/sub | solution.py:70
  219.9 5.1 %exponential_reduce_fusion.2 = (f32[2,2,256]{2,1,0:T(2,128)S(1)}, f32[2,2,256,1280]{3,2,1,0:T(8,128)}) fusion(pred[256,1280]{1,0:T(8,128)(4,1)S(1)} %fusion.80, bf16[2,3072,128]{2,1,0:T(8,128)(2,1)S(1)} %get-tuple-element.369, s32[]{:T(128)S(6)} %select_n.30, bf16[2,2,2048,128]{3,2,1,0:T(8,128)(2,1)} %get-tuple-element.368, s32[]{:T(128)S(6)} %select_n.29), kind=kOutput, calls=%fused_computation.5.clone.1 | convolution fusion | flops 340788480 | bytes 6492168 | tf_op jit(solution)/shard_map/while/body/eval_jaxpr/sub | solution.py:70
  319.5 8.4 %slice_bitcast_fusion.4 = (f32[8,2,256,128]{3,2,1,0:T(8,128)S(1)}, f32[8,2,256,128]{3,2,1,0:T(8,128)}, f32[8,2,256,128]{3,2,1,0:T(8,128)}, f32[8,2,256,128]{3,2,1,0:T(8,128)}, f32[8,2,256,128]{3,2,1,0:T(8,128)}) fusion(f32[8,2,5,256,128]{4,3,2,1,0:T(8,128)} %bitcast.194), kind=kLoop, calls=%fused_computation.51 | loop fusion | bytes 20971520 | tf_op jit(solution)/shard_map/squeeze | solution.py:27
  327.9 6.3 %fusion.39 = (bf16[12,256,2,128]{3,1,2,0:T(8,128)(2,1)S(1)}, f32[12,256,2,128]{3,1,2,0:T(8,128)}) fusion(f32[8,2,256,128]{3,2,1,0:T(8,128)} %get-tuple-element.234, f32[8,2,256,128]{3,2,1,0:T(8,128)} %get-tuple-element.235, f32[8,2,256,128]{3,2,1,0:T(8,128)} %get-tuple-element.232, f32[8,2,256,128]{3,2,1,0:T(8,128)} %get-tuple-element.233, ...), kind=kLoop, calls=%fused_computation.65 | loop fusion | flops 3932160 | bytes 15204352 | tf_op jit(solution)/shard_map/convert.3
  349.7 9.5 %copy.123 = bf16[2048,2,128]{2,1,0:T(2,128)(2,1)} copy(bf16[2048,2,128]{2,0,1:T(8,128)(2,1)S(1)} %pad_maximum_fusion.1) | data formatting | bytes 2097152 | tf_op jit(solution)/shard_map/concatenate | solution.py:139
  359.2 5.7 %all-to-all-start.7 = ((bf16[2048,2,128]{2,1,0:T(2,128)(2,1)}), bf16[2048,2,128]{2,1,0:T(2,128)(2,1)S(1)}, u32[]{:S(2)}, u32[]{:S(2)}) async-start(bf16[2048,2,128]{2,1,0:T(2,128)(2,1)} %copy.123), calls=%async_computation.7 | async-start | bytes 2097152 | tf_op jit(solution)/shard_map/all_to_all | solution.py:146
  367.6 9.5 %copy.113 = bf16[2048,2,128]{2,1,0:T(2,128)(2,1)} copy(bf16[2048,2,128]{2,0,1:T(8,128)(2,1)S(1)} %pad_maximum_fusion) | data formatting | bytes 2097152 | tf_op jit(solution)/shard_map/concatenate | solution.py:136
  377.6 6.5 %all-to-all-start.6 = ((bf16[2048,2,128]{2,1,0:T(2,128)(2,1)}), bf16[2048,2,128]{2,1,0:T(2,128)(2,1)S(1)}, u32[]{:S(2)}, u32[]{:S(2)}) async-start(bf16[2048,2,128]{2,1,0:T(2,128)(2,1)} %copy.113), calls=%async_computation.6 | async-start | bytes 2097152 | tf_op jit(solution)/shard_map/all_to_all | solution.py:145
  388.7 8.0 %all-to-all-done.6 = bf16[2048,2,128]{2,1,0:T(2,128)(2,1)S(1)} async-done(((bf16[2048,2,128]{2,1,0:T(2,128)(2,1)}), bf16[2048,2,128]{2,1,0:T(2,128)(2,1)S(1)}, u32[]{:S(2)}, u32[]{:S(2)}) %all-to-all-start.6) | async-done | bytes 1048608 | tf_op jit(solution)/shard_map/all_to_all | solution.py:145
  397.7 6.3 %all-to-all-start.4 = ((bf16[2048,4,128]{2,1,0:T(4,128)(2,1)}), bf16[2048,4,128]{2,1,0:T(4,128)(2,1)S(1)}, u32[]{:S(2)}, u32[]{:S(2)}) async-start(bf16[2048,4,128]{2,1,0:T(4,128)(2,1)} %copy.99), calls=%async_computation.4 | async-start | bytes 4194304 | tf_op jit(solution)/shard_map/all_to_all | solution.py:143
  408.6 19.3 %all-to-all-done.4 = bf16[2048,4,128]{2,1,0:T(4,128)(2,1)S(1)} async-done(((bf16[2048,4,128]{2,1,0:T(4,128)(2,1)}), bf16[2048,4,128]{2,1,0:T(4,128)(2,1)S(1)}, u32[]{:S(2)}, u32[]{:S(2)}) %all-to-all-start.4) | async-done | bytes 2097184 | tf_op jit(solution)/shard_map/all_to_all | solution.py:143
  427.9 7.0 %all-to-all-start.5 = ((bf16[2048,4,128]{2,1,0:T(4,128)(2,1)}), bf16[2048,4,128]{2,1,0:T(4,128)(2,1)}, u32[]{:S(2)}, u32[]{:S(2)}) async-start(bf16[2048,4,128]{2,1,0:T(4,128)(2,1)} %copy.103), calls=%async_computation.5 | async-start | bytes 4194304 | tf_op jit(solution)/shard_map/all_to_all | solution.py:144
  451.9 6.9 %all-to-all-done.5 = bf16[2048,4,128]{2,1,0:T(4,128)(2,1)} async-done(((bf16[2048,4,128]{2,1,0:T(4,128)(2,1)}), bf16[2048,4,128]{2,1,0:T(4,128)(2,1)}, u32[]{:S(2)}, u32[]{:S(2)}) %all-to-all-start.5) | async-done | bytes 2097184 | tf_op jit(solution)/shard_map/all_to_all | solution.py:144
  (281 shorter events, 271.6 us)
Async XLA Ops:
  0.6 6.9 %copy-start.9 = (bf16[256,2048]{1,0:T(8,128)(2,1)S(1)}, bf16[256,2048]{1,0:T(8,128)(2,1)}, u32[]{:S(2)}) copy-start(bf16[256,2048]{1,0:T(8,128)(2,1)} %param.8) | copy-start | bytes 3145732
  3.0 17.2 %all-to-all-start.1 = ((bf16[256,16,128]{0,2,1:T(8,128)(2,1)}), bf16[256,16,128]{0,2,1:T(8,128)(2,1)S(1)}, u32[]{:S(2)}, u32[]{:S(2)}) async-start(bf16[256,16,128]{0,2,1:T(8,128)(2,1)} %bitcast.21), calls=%async_computation.1 | async-start | bytes 2097152 | tf_op jit(solution)/shard_map/all_to_all | solution.py:118
  20.2 18.9 %all-to-all-start.2 = ((bf16[256,16,128]{0,2,1:T(8,128)(2,1)}), bf16[256,16,128]{0,2,1:T(8,128)(2,1)S(1)}, u32[]{:S(2)}, u32[]{:S(2)}) async-start(bf16[256,16,128]{0,2,1:T(8,128)(2,1)} %bitcast.29), calls=%async_computation.2 | async-start | bytes 2097152 | tf_op jit(solution)/shard_map/all_to_all | solution.py:119
  39.1 31.0 %all-to-all-start = ((bf16[256,32,128]{0,2,1:T(8,128)(2,1)}), bf16[256,32,128]{0,2,1:T(8,128)(2,1)}, u32[]{:S(2)}, u32[]{:S(2)}) async-start(bf16[256,32,128]{0,2,1:T(8,128)(2,1)} %bitcast.201), calls=%async_computation | async-start | bytes 4194304 | tf_op jit(solution)/shard_map/all_to_all | solution.py:117
  70.1 40.4 %all-to-all-start.3 = ((bf16[256,32,128]{0,2,1:T(8,128)(2,1)}), bf16[256,32,128]{0,2,1:T(8,128)(2,1)}, u32[]{:S(2)}, u32[]{:S(2)}) async-start(bf16[256,32,128]{0,2,1:T(8,128)(2,1)} %bitcast.200), calls=%async_computation.3 | async-start | bytes 4194304 | tf_op jit(solution)/shard_map/all_to_all | solution.py:120
  78.7 14.4 %collective-permute-start = (bf16[1024,2,128]{2,0,1:T(8,128)(2,1)}, bf16[1024,2,128]{2,0,1:T(8,128)(2,1)}, u32[]{:S(2)}, u32[]{:S(2)}) collective-permute-start(bf16[1024,2,128]{2,0,1:T(8,128)(2,1)} %bitcast.24), channel_id=1, source_target_pairs={{0,8},{8,16},{16,24},{1,9},{9,17},{17,25},{2,10},{10,18},{18,26},{... | collective-permute-start | bytes 1572872 | tf_op jit(solution)/shard_map/ppermute | solution.py:17
  84.2 20.2 %collective-permute-start.1 = (bf16[1024,2,128]{2,0,1:T(8,128)(2,1)}, bf16[1024,2,128]{2,0,1:T(8,128)(2,1)}, u32[]{:S(2)}, u32[]{:S(2)}) collective-permute-start(bf16[1024,2,128]{2,0,1:T(8,128)(2,1)} %bitcast.32), channel_id=1, source_target_pairs={{0,8},{8,16},{16,24},{1,9},{9,17},{17,25},{2,10},{10,18},{18,26},{... | collective-permute-start | bytes 1572872 | tf_op jit(solution)/shard_map/ppermute | solution.py:17
  114.5 8.1 %copy-start.3 = (bf16[2,3072,128]{2,1,0:T(8,128)(2,1)}, bf16[2,3072,128]{2,1,0:T(8,128)(2,1)S(1)}, u32[]{:S(2)}) copy-start(bf16[2,3072,128]{2,1,0:T(8,128)(2,1)S(1)} %get-tuple-element.369) | copy-start | bytes 4718596 | tf_op jit(solution)/shard_map/while
  140.0 8.1 %copy-start.3 = (bf16[2,3072,128]{2,1,0:T(8,128)(2,1)}, bf16[2,3072,128]{2,1,0:T(8,128)(2,1)S(1)}, u32[]{:S(2)}) copy-start(bf16[2,3072,128]{2,1,0:T(8,128)(2,1)S(1)} %get-tuple-element.369) | copy-start | bytes 4718596 | tf_op jit(solution)/shard_map/while
  165.7 8.1 %copy-start.3 = (bf16[2,3072,128]{2,1,0:T(8,128)(2,1)}, bf16[2,3072,128]{2,1,0:T(8,128)(2,1)S(1)}, u32[]{:S(2)}) copy-start(bf16[2,3072,128]{2,1,0:T(8,128)(2,1)S(1)} %get-tuple-element.369) | copy-start | bytes 4718596 | tf_op jit(solution)/shard_map/while
  191.3 8.1 %copy-start.3 = (bf16[2,3072,128]{2,1,0:T(8,128)(2,1)}, bf16[2,3072,128]{2,1,0:T(8,128)(2,1)S(1)}, u32[]{:S(2)}) copy-start(bf16[2,3072,128]{2,1,0:T(8,128)(2,1)S(1)} %get-tuple-element.369) | copy-start | bytes 4718596 | tf_op jit(solution)/shard_map/while
  217.0 8.1 %copy-start.3 = (bf16[2,3072,128]{2,1,0:T(8,128)(2,1)}, bf16[2,3072,128]{2,1,0:T(8,128)(2,1)S(1)}, u32[]{:S(2)}) copy-start(bf16[2,3072,128]{2,1,0:T(8,128)(2,1)S(1)} %get-tuple-element.369) | copy-start | bytes 4718596 | tf_op jit(solution)/shard_map/while
  242.6 8.1 %copy-start.3 = (bf16[2,3072,128]{2,1,0:T(8,128)(2,1)}, bf16[2,3072,128]{2,1,0:T(8,128)(2,1)S(1)}, u32[]{:S(2)}) copy-start(bf16[2,3072,128]{2,1,0:T(8,128)(2,1)S(1)} %get-tuple-element.369) | copy-start | bytes 4718596 | tf_op jit(solution)/shard_map/while
  268.2 8.1 %copy-start.3 = (bf16[2,3072,128]{2,1,0:T(8,128)(2,1)}, bf16[2,3072,128]{2,1,0:T(8,128)(2,1)S(1)}, u32[]{:S(2)}) copy-start(bf16[2,3072,128]{2,1,0:T(8,128)(2,1)S(1)} %get-tuple-element.369) | copy-start | bytes 4718596 | tf_op jit(solution)/shard_map/while
  293.9 8.1 %copy-start.3 = (bf16[2,3072,128]{2,1,0:T(8,128)(2,1)}, bf16[2,3072,128]{2,1,0:T(8,128)(2,1)S(1)}, u32[]{:S(2)}) copy-start(bf16[2,3072,128]{2,1,0:T(8,128)(2,1)S(1)} %get-tuple-element.369) | copy-start | bytes 4718596 | tf_op jit(solution)/shard_map/while
  319.5 16.4 %slice-start = ((s8[10485760]{0:T(1024)(128)(4,1)}), s8[4194304]{0:T(1024)(128)(4,1)S(1)}, s32[]{:S(2)}) async-start(s8[10485760]{0:T(1024)(128)(4,1)} %bitcast.195), calls=%async_computation.8 | async-start | bytes 8388608
  319.5 16.4 %slice-start.1 = ((s8[10485760]{0:T(1024)(128)(4,1)}), s8[4194304]{0:T(1024)(128)(4,1)S(1)}, s32[]{:S(2)}) async-start(s8[10485760]{0:T(1024)(128)(4,1)} %bitcast.195), calls=%async_computation.9 | async-start | bytes 8388608
  327.9 8.0 %slice-start.2 = ((s8[10485760]{0:T(1024)(128)(4,1)}), s8[2097152]{0:T(1024)(128)(4,1)S(1)}, s32[]{:S(2)}) async-start(s8[10485760]{0:T(1024)(128)(4,1)} %bitcast.195), calls=%async_computation.10 | async-start | bytes 4194304
  334.4 15.1 %collective-permute-start.3 = (bf16[1024,2,128]{2,0,1:T(8,128)(2,1)S(1)}, bf16[1024,2,128]{2,0,1:T(8,128)(2,1)S(1)}, u32[]{:S(2)}, u32[]{:S(2)}) collective-permute-start(bf16[1024,2,128]{2,0,1:T(8,128)(2,1)S(1)} %bitcast.220), channel_id=1, source_target_pairs={{8,0},{16,8},{24,16},{9,1},{17,9},{25,17},{10,2},{18,10},{26,18},{... | collective-permute-start | bytes 1572872 | tf_op jit(solution)/shard_map/ppermute | solution.py:17
  346.8 19.4 %collective-permute-start.2 = (bf16[1024,2,128]{2,0,1:T(8,128)(2,1)S(1)}, bf16[1024,2,128]{2,0,1:T(8,128)(2,1)}, u32[]{:S(2)}, u32[]{:S(2)}) collective-permute-start(bf16[1024,2,128]{2,0,1:T(8,128)(2,1)S(1)} %bitcast.221), channel_id=1, source_target_pairs={{8,0},{16,8},{24,16},{9,1},{17,9},{25,17},{10,2},{18,10},{26,18},{... | collective-permute-start | bytes 1572872 | tf_op jit(solution)/shard_map/ppermute | solution.py:17
  359.2 18.4 %all-to-all-start.7 = ((bf16[2048,2,128]{2,1,0:T(2,128)(2,1)}), bf16[2048,2,128]{2,1,0:T(2,128)(2,1)S(1)}, u32[]{:S(2)}, u32[]{:S(2)}) async-start(bf16[2048,2,128]{2,1,0:T(2,128)(2,1)} %copy.123), calls=%async_computation.7 | async-start | bytes 2097152 | tf_op jit(solution)/shard_map/all_to_all | solution.py:146
  377.6 19.1 %all-to-all-start.6 = ((bf16[2048,2,128]{2,1,0:T(2,128)(2,1)}), bf16[2048,2,128]{2,1,0:T(2,128)(2,1)S(1)}, u32[]{:S(2)}, u32[]{:S(2)}) async-start(bf16[2048,2,128]{2,1,0:T(2,128)(2,1)} %copy.113), calls=%async_computation.6 | async-start | bytes 2097152 | tf_op jit(solution)/shard_map/all_to_all | solution.py:145
  397.7 30.2 %all-to-all-start.4 = ((bf16[2048,4,128]{2,1,0:T(4,128)(2,1)}), bf16[2048,4,128]{2,1,0:T(4,128)(2,1)S(1)}, u32[]{:S(2)}, u32[]{:S(2)}) async-start(bf16[2048,4,128]{2,1,0:T(4,128)(2,1)} %copy.99), calls=%async_computation.4 | async-start | bytes 4194304 | tf_op jit(solution)/shard_map/all_to_all | solution.py:143
  427.9 31.0 %all-to-all-start.5 = ((bf16[2048,4,128]{2,1,0:T(4,128)(2,1)}), bf16[2048,4,128]{2,1,0:T(4,128)(2,1)}, u32[]{:S(2)}, u32[]{:S(2)}) async-start(bf16[2048,4,128]{2,1,0:T(4,128)(2,1)} %copy.103), calls=%async_computation.5 | async-start | bytes 4194304 | tf_op jit(solution)/shard_map/all_to_all | solution.py:144
  (36 other events, 124.5 us)
where the time goes:
time: 473 us; the launch traced here: 467 us
  matrix products  143 us (30%)
  local copies, waits for them, and re-layouts  117 us (25%)
  waiting for transfers between devices  89.7 us (19%)
  starting transfers between devices  60.1 us (13%)
  other arithmetic  50.5 us (11%)
  loops' own time  5.99 us (1%)
    sub x8, matrix products, block_step(): unnormed = jnp.exp(scores - largest)  41.1 us
    convert_element_type x8, other arithmetic, block_step(): probs_low = probs.astype(jnp.bfloat16)  30.8 us
    dot_general x8, matrix products, block_step(): jnp.einsum('sgqk,skd->sgqd', grad_scores, key_stack, preferred_element_ty...  27.4 us
    dot_general x8, matrix products, block_step(): jnp.einsum('sgqk,sgqd->skd', grad_scores, query_stack, preferred_element_...  26.6 us
    unnamed x24, local copies, waits for them, and re-layouts  24.4 us
    dot_general x8, matrix products, block_step(): jnp.einsum('sgqd,skd->sgqk', grad_stack, value_stack, preferred_element_t...  22.1 us
    all_to_all x1, waiting for transfers between devices, body(): lax.all_to_all(query_rows, 'head', split_axis=1, concat_axis=0, tiled=True)  20 us
    all_to_all x1, waiting for transfers between devices, body(): lax.all_to_all(attended_group, 'head', split_axis=0, concat_axis=1, tiled...  19.3 us
  transfers between devices with their start and end apart: 12, of which 10 were waited for; matrix products, arithmetic and copies ran while one was open for 17% of the time, Pallas kernels for 0%

commit v1 on v0

v1 whole, which is shorter than its diff:
```python
import functools

import jax
import jax.numpy as jnp
from jax import lax
from jax.experimental import pallas as pl
from jax.experimental.pallas import tpu as pltpu
from jax.sharding import PartitionSpec as P

HD = 128
WIN = 1024
QPRE = 168
SCALE = QPRE ** -0.5
LOG2E = 1.4426950408889634
FAR = 1e30
MESH = pl.DeviceIdType.MESH


def contract(a, b):
    return jnp.dot(a, b, preferred_element_type=jnp.float32)


def kernel(
    chips, head_size,
    q_in, k_in, v_in, g_in, o_out, dq_out, dk_out, dv_out,
    qg, kv, obuf, dqbuf, part, relay, back, own, final,
    qg_sem, kv_sem, relay_sem, back_sem, out_recv, out_local,
    near_send, one_send, two_send, fwd_send, part_send, out_send,
):
    rows = q_in.shape[0]
    heads = qg.shape[0]
    width = qg.shape[4]
    linear = lax.axis_index("ctx") * head_size + lax.axis_index("head")
    chip = linear // 2
    core = linear % 2
    other = 1 - core
    odd = chip % 2
    has_one = chip >= 1
    has_two = chip >= 2
    to_one = chip + 1 < chips
    to_two = chip + 2 < chips

    def device(c, k):
        index = c * 2 + k
        return (index // head_size, index % head_size)

    def remote(src, dst, send, recv, c, k):
        return pltpu.make_async_remote_copy(
            src_ref=src, dst_ref=dst, send_sem=send, recv_sem=recv,
            device_id=device(c, k), device_id_type=MESH,
        )

    def drain(ref, sem):
        pltpu.make_async_copy(ref, ref, sem).wait()

    barrier = pltpu.get_barrier_semaphore()
    pl.semaphore_signal(barrier, inc=1, device_id=device(chip, other), device_id_type=MESH)
    for step, there in ((-2, has_two), (-1, has_one), (1, to_one), (2, to_two)):
        @pl.when(there)
        def _():
            for k in (0, 1):
                pl.semaphore_signal(barrier, inc=1, device_id=device(chip + step, k), device_id_type=MESH)
    greeted = (1 + 2 * jnp.minimum(chip, 2) + 2 * jnp.minimum(chips - 1 - chip, 2)).astype(jnp.int32)
    pl.semaphore_wait(barrier, greeted)

    def send_head(h, carry):
        for half in (0, 1):
            column = half * heads + h
            narrow = pl.ds(pl.multiple_of(column * HD, HD), HD)
            wide = pl.ds(pl.multiple_of(column * width, width), width)
            pairs = [(ref.at[:, narrow], i) for i, ref in enumerate((k_in, v_in))]
            wides = [(ref.at[:, wide], i) for i, ref in enumerate((q_in, g_in))]

            @pl.when(to_two)
            def _():
                for src, i in pairs:
                    remote(src, kv.at[h, i, core], two_send, kv_sem.at[h, 0], chip + 2, half).start()

            @pl.when(to_one & (odd == 0))
            def _():
                for src, i in pairs:
                    remote(src, kv.at[h, i, 2 + core], one_send, kv_sem.at[h, 1], chip + 1, half).start()

            @pl.when(core == half)
            def _():
                for src, i in pairs:
                    pltpu.make_async_copy(src, kv.at[h, i, 4 + core], kv_sem.at[h, 2]).start()
                for src, i in wides:
                    pltpu.make_async_copy(src, qg.at[h, i, core], qg_sem.at[h]).start()

            @pl.when(core != half)
            def _():
                for src, i in pairs:
                    remote(src, kv.at[h, i, 4 + core], near_send.at[0], kv_sem.at[h, 2], chip, half).start()
                for src, i in wides:
                    remote(src, qg.at[h, i, core], near_send.at[1], qg_sem.at[h], chip, half).start()
        return carry

    lax.fori_loop(0, heads, send_head, 0)

    for slot, there in ((0, has_two), (1, has_one)):
        @pl.when(jnp.logical_not(there))
        def _():
            for i in (0, 1):
                for b in (0, 1):
                    kv[:, i, 2 * slot + b] = jnp.zeros((heads, rows, HD), jnp.bfloat16)

    sub = lax.broadcasted_iota(jnp.int32, (rows, 2 * rows), 0)
    lane = lax.broadcasted_iota(jnp.int32, (rows, 2 * rows), 1)
    early = sub > jnp.where(lane >= rows, lane - rows, lane)
    valid = {0: has_two, 1: has_one}
    far_bias = jnp.where(has_two, 0.0, -FAR)

    def compute(h):
        grads = {}
        for t in (0, 1):
            q2, g2 = qg[h, 0, t], qg[h, 1, t]
            qt = jnp.concatenate([q2[:, :HD].T, q2[:, HD:].T], axis=1)
            gt = jnp.concatenate([g2[:, :HD].T, g2[:, HD:].T], axis=1)
            keys = [kv[h, 0, t + b] for b in range(5)]
            vals = [kv[h, 1, t + b] for b in range(5)]
            raw = [contract(k, qt) for k in keys]
            scores = [jnp.where(early, raw[0] + far_bias, raw[4])] + raw[1:4]
            slots = [2] + [(t + b) // 2 for b in (1, 2, 3)]
            tops = []
            for s, slot in zip(scores, slots):
                top = jnp.max(s, axis=0, keepdims=True)
                tops.append(jnp.where(valid[slot], top, -FAR) if slot < 2 else top)
            top = functools.reduce(jnp.maximum, tops) * (SCALE * LOG2E)
            probs, total = [], None
            for s, slot in zip(scores, slots):
                less = jnp.where(valid[slot], top, FAR) if slot < 2 else top
                p = jnp.exp2(s * (SCALE * LOG2E) - less)
                summed = jnp.sum(p, axis=0, keepdims=True)
                total = summed if total is None else total + summed
                probs.append(p.astype(jnp.bfloat16))
            inverse = 1.0 / total
            nothing = jnp.zeros_like(probs[0])

            def spread(items):
                return [jnp.where(early, items[0], nothing)] + items[1:] + [jnp.where(early, nothing, items[0])]

            low = spread(probs)
            out = functools.reduce(jnp.add, [contract(v.T, p) for v, p in zip(vals, low)]) * inverse
            out_low = out.astype(jnp.bfloat16)
            grad = gt.astype(jnp.float32)
            inner = jnp.sum(grad * out_low.astype(jnp.float32), axis=0, keepdims=True)
            dp = [contract(v, gt) for v in vals]
            dp = [jnp.where(early, dp[0], dp[4])] + dp[1:4]
            ds = spread([(p.astype(jnp.float32) * (d - inner)).astype(jnp.bfloat16) for p, d in zip(probs, dp)])
            dq = functools.reduce(jnp.add, [contract(k.T, d) for k, d in zip(keys, ds)]) * (inverse * SCALE)
            dq_low = dq.astype(jnp.bfloat16)
            for i in (0, 1):
                lanes = slice(i * rows, (i + 1) * rows)
                obuf[h, t, :, i * HD:(i + 1) * HD] = out_low[:, lanes].T
                dqbuf[h, t, :, i * HD:(i + 1) * HD] = dq_low[:, lanes].T
            gn = (grad * inverse).astype(jnp.bfloat16).T
            qn = (qt.astype(jnp.float32) * (inverse * SCALE)).astype(jnp.bfloat16).T
            for b in range(5):
                for i, term in ((0, contract(ds[b], qn)), (1, contract(low[b], gn))):
                    place = (i, t + b)
                    grads[place] = term if place not in grads else grads[place] + term
        for i in (0, 1):
            for b in range(4):
                part[h, b // 2, i, b % 2] = grads[i, b].astype(jnp.bfloat16)
            for b in (4, 5):
                own[h, i, b - 4] = grads[i, b]

    def hand_out(src, out, column, columns, number):
        cols = pl.ds(pl.multiple_of(column * columns, columns), columns)
        for t in (0, 1):
            @pl.when(core == t)
            def _():
                pltpu.make_async_copy(src.at[t], out.at[:, cols], out_local.at[number]).start()

            @pl.when(core != t)
            def _():
                remote(src.at[t], out.at[:, cols], out_send.at[number], out_recv.at[number], chip, t).start()

    def merge(h):
        @pl.when((odd == 1) & has_two)
        def _():
            drain(relay.at[h], relay_sem.at[h])
            part[h, 0] = (part[h, 0].astype(jnp.float32) + relay[h].astype(jnp.float32)).astype(jnp.bfloat16)
            remote(part.at[h, 0], back.at[h, 0], part_send.at[h, 0], back_sem.at[h, 0], chip - 2, core).start()

    def step(h, carry):
        drain(kv.at[h, :, 4:6], kv_sem.at[h, 2])
        drain(qg.at[h], qg_sem.at[h])

        @pl.when(has_two)
        def _():
            drain(kv.at[h, :, 0:2], kv_sem.at[h, 0])

        @pl.when((odd == 1) & has_two)
        def _():
            remote(kv.at[h, :, 0:2], kv.at[h, :, 2:4], fwd_send.at[h], kv_sem.at[h, 1], chip - 1, core).start()

        @pl.when(has_one)
        def _():
            drain(kv.at[h, :, 2:4], kv_sem.at[h, 1])

        compute(h)

        @pl.when((odd == 0) & has_two)
        def _():
            remote(part.at[h, 1], relay.at[h], part_send.at[h, 1], relay_sem.at[h], chip + 1, core).start()
            remote(part.at[h, 0], back.at[h, 0], part_send.at[h, 0], back_sem.at[h, 0], chip - 2, core).start()

        @pl.when(odd == 1)
        def _():
            remote(part.at[h, 1], back.at[h, 1], part_send.at[h, 1], back_sem.at[h, 1], chip - 1, core).start()

        @pl.when(h >= 1)
        def _():
            merge(jnp.maximum(h - 1, 0))

        column = core * heads + h
        hand_out(obuf.at[h], o_out, column, width, 0)
        hand_out(dqbuf.at[h], dq_out, column, width, 1)
        return carry

    lax.fori_loop(0, heads, step, 0)
    merge(heads - 1)

    def finish(h, carry):
        @pl.when(to_two)
        def _():
            drain(back.at[h, 0], back_sem.at[h, 0])
            own[h] = own[h] + back[h, 0].astype(jnp.float32)

        @pl.when(odd == 0)
        def _():
            drain(back.at[h, 1], back_sem.at[h, 1])
            own[h] = own[h] + back[h, 1].astype(jnp.float32)

        final[h] = own[h].astype(jnp.bfloat16)
        column = core * heads + h
        hand_out(final.at[h, 0], dk_out, column, HD, 2)
        hand_out(final.at[h, 1], dv_out, column, HD, 3)
        return carry

    lax.fori_loop(0, heads, finish, 0)

    half_kv = k_in.shape[1] // 2
    half_q = q_in.shape[1] // 2
    for number, ref, size in ((0, o_out, half_q), (1, dq_out, half_q), (2, dk_out, half_kv), (3, dv_out, half_kv)):
        for sems in (out_local, out_send, out_recv):
            drain(ref.at[:, 0:size], sems.at[number])
    drain(k_in, near_send.at[0])
    drain(q_in, near_send.at[1])

    @pl.when(to_two)
    def _():
        drain(k_in, two_send)
        drain(v_in, two_send)

    @pl.when(to_one & (odd == 0))
    def _():
        drain(k_in, one_send)
        drain(v_in, one_send)

    def sent(h, carry):
        @pl.when(has_two)
        def _():
            drain(part.at[h, 0], part_send.at[h, 0])

        @pl.when((odd == 1) | has_two)
        def _():
            drain(part.at[h, 1], part_send.at[h, 1])

        @pl.when((odd == 1) & has_two)
        def _():
            drain(kv.at[h, :, 0:2], fwd_send.at[h])
        return carry

    lax.fori_loop(0, heads, sent, 0)


def body(head_size, chips, queries, keys, values, grad_out):
    rows = queries.shape[0]
    heads = keys.shape[1] // HD // 2
    width = queries.shape[1] // (2 * heads)
    assert rows * 4 == WIN and width == 2 * HD
    low, full = jnp.bfloat16, jnp.float32
    dma = pltpu.SemaphoreType.DMA
    anywhere = pl.BlockSpec(memory_space=pl.ANY)
    flops = 12 * rows * (queries.shape[1] // HD) * (WIN + rows) * HD
    return pl.pallas_call(
        functools.partial(kernel, chips, head_size),
        out_shape=tuple(jax.ShapeDtypeStruct(a.shape, low) for a in (queries, queries, keys, keys)),
        in_specs=[anywhere] * 4,
        out_specs=(anywhere,) * 4,
        scratch_shapes=[
            pltpu.VMEM((heads, 2, 2, rows, width), low),
            pltpu.VMEM((heads, 2, 6, rows, HD), low),
            pltpu.VMEM((heads, 2, rows, width), low),
            pltpu.VMEM((heads, 2, rows, width), low),
            pltpu.VMEM((heads, 2, 2, 2, rows, HD), low),
            pltpu.VMEM((heads, 2, 2, rows, HD), low),
            pltpu.VMEM((heads, 2, 2, 2, rows, HD), low),
            pltpu.VMEM((heads, 2, 2, rows, HD), full),
            pltpu.VMEM((heads, 2, 2, rows, HD), low),
            dma((heads,)), dma((heads, 3)), dma((heads,)), dma((heads, 2)), dma((4,)), dma((4,)),
            dma((2,)), dma(()), dma(()), dma((heads,)), dma((heads, 2)), dma((4,)),
        ],
        cost_estimate=pl.CostEstimate(flops=flops, bytes_accessed=12 * 2 ** 20, transcendentals=flops // 1536),
        compiler_params=pltpu.CompilerParams(
            collective_id=0, has_side_effects=True, vmem_limit_bytes=56 * 2 ** 20
        ),
    )(queries, keys, values, grad_out)


def solution(mesh):
    head_size = mesh.shape["head"]
    chips = mesh.shape["ctx"] * head_size // 2
    placed = (P(("ctx", "head"), None),) * 4
    return jax.shard_map(
        functools.partial(body, head_size, chips), mesh=mesh, in_specs=placed, out_specs=placed, check_vma=False
    )
```

time: 473 us -> 147 us (0.31); the launches traced: 467 us -> 147 us
  matrix products: 143 us -> 0 us
  Pallas kernels: 0 us -> 138 us
  local copies, waits for them, and re-layouts: 117 us -> 7.81 us
  waiting for transfers between devices: 89.7 us -> 0 us
  starting transfers between devices: 60.1 us -> 0 us
  other arithmetic: 50.5 us -> 0 us
  loops' own time: 5.99 us -> 0 us
    pallas_call x0 -> x1, Pallas kernels: none -> 138 us  [body(): pl.pallas_call(functools.partial(kernel, chips, head_size), out_shape=tup...]
    dot_general x40 -> x0, matrix products: 102 us -> none  [the longest x8 27.4 us: block_step(): jnp.einsum('sgqk,skd->sgqd', grad_scores, key_stack, preferred_element_ty...]
    all_to_all x8 -> x0, waiting for transfers between devices: 74.8 us -> none  [the longest x1 20 us: body(): lax.all_to_all(query_rows, 'head', split_axis=1, concat_axis=0, tiled=True)]
    all_to_all x8 -> x0, starting transfers between devices: 50.1 us -> none  [the longest x1 7 us: body(): lax.all_to_all(grad_rows, 'head', split_axis=1, concat_axis=0, tiled=True)]
    sub x8 -> x0, matrix products: 41.1 us -> none  [block_step(): unnormed = jnp.exp(scores - largest)]
    convert_element_type x8 -> x0, other arithmetic: 30.8 us -> none  [block_step(): probs_low = probs.astype(jnp.bfloat16)]
    all_to_all x14 -> x0, local copies, waits for them, and re-layouts: 26.1 us -> none  [the longest x2 4.47 us: body(): lax.all_to_all(grad_query_group, 'head', split_axis=0, concat_axis=1, til...]
    concatenate x2 -> x0, local copies, waits for them, and re-layouts: 18.9 us -> none  [the longest x1 9.46 us: body(): jnp.concatenate([key_total[WIN:group_rows], key_total[group_rows:] + key_...]
  transfers between devices with their start and end apart: 12 -> 0, of which waited for: 10 -> 0; matrix products, arithmetic and copies ran while one was open for 17% -> 0% of each run, Pallas kernels for 0% -> 0%
where the time goes in v1:
time: 147 us
  Pallas kernels  138 us (94%)
  local copies, waits for them, and re-layouts  7.81 us (5%)
    pallas_call x1, Pallas kernels, body(): pl.pallas_call(functools.partial(kernel, chips, head_size), out_shape=tup...  138 us
    unnamed x10, local copies, waits for them, and re-layouts  7.81 us

profile of v1, /device:TPU:7, one launch (start us, length us, event | category | flops | bytes accessed | tf_op | source)
XLA Modules:
  0.0 146.8 jit_solution(12495696390468574228)
XLA Ops:
  0.6 138.4 %shard_map.75 = (bf16[256,4096]{1,0:T(8,128)(2,1)}, bf16[256,4096]{1,0:T(8,128)(2,1)}, bf16[256,2048]{1,0:T(8,128)(2,1)}, bf16[256,2048]{1,0:T(8,128)(2,1)}) custom-call(bf16[256,4096]{1,0:T(8,128)(2,1)} %q_in.1, bf16[256,2048]{1,0:T(8,128)(2,1)} %k_in.1, bf16[256,2048]{1,0:T(8,128)(2,1)} %v_in.1, bf16[256,4096]{1,0:T(8,128)(2,1)} %g_in.1), custom_call_target="tpu_custom_call" | custom-call | flops 16106127360 | bytes 12582912 | tf_op jit(solution)/shard_map/pallas_call | solution.py:289
  139.0 0.0 copy-start
  139.0 3.3 %copy.12 = bf16[256,4096]{1,0:T(8,128)(2,1)} copy(bf16[256,4096]{1,0:T(8,128)(2,1)} %get-tuple-element.8) | data formatting | bytes 4194304
  142.3 0.0 copy-done
  142.3 0.0 copy-start.2
  142.3 1.3 copy.13
  143.6 0.6 copy-done.2
  144.3 0.0 copy-start.1
  144.3 1.0 copy.14
  145.2 0.6 copy-done.1
  145.9 1.0 copy.15
Async XLA Ops:
  139.0 3.3 %copy-start = (bf16[256,4096]{1,0:T(8,128)(2,1)S(1)}, bf16[256,4096]{1,0:T(8,128)(2,1)}, u32[]{:S(2)}) copy-start(bf16[256,4096]{1,0:T(8,128)(2,1)} %get-tuple-element.9) | copy-start | bytes 6291460
  142.3 2.0 %copy-start.2 = (bf16[256,2048]{1,0:T(8,128)(2,1)S(1)}, bf16[256,2048]{1,0:T(8,128)(2,1)}, u32[]{:S(2)}) copy-start(bf16[256,2048]{1,0:T(8,128)(2,1)} %get-tuple-element.10) | copy-start | bytes 3145732
  144.3 1.6 %copy-start.1 = (bf16[256,2048]{1,0:T(8,128)(2,1)S(1)}, bf16[256,2048]{1,0:T(8,128)(2,1)}, u32[]{:S(2)}) copy-start(bf16[256,2048]{1,0:T(8,128)(2,1)} %get-tuple-element.11) | copy-start | bytes 3145732
